TPU v7x, 128 devices: a whole 4x4x4 slice. The times are simulated.
128 devices in a mesh: row: 8 (over x, core), col: 16 (over z, y).
Axes of the slice: x: 4, y: 4, z: 4, core: 2. Of those that a mesh axis runs over, the one named last changes fastest.
Arguments:
- density: bfloat16 [6144, 6144], P('row', 'col'), may hold values from -5 to 5
- strips: bfloat16 [16384, 8, 128], P(('row', 'col')), may hold values from -5 to 5
- dest_device: int32 [16384, 1], P(('row', 'col')), may hold values from 0 to 127; in each aligned block of 128 rows (0 to 127, 128 to 255, ...) at most 2 rows name the same one
- atom_slot: int32 [16384], P(('row', 'col')), may hold values from 0 to 95
- block_slot: int32 [16384], P(('row', 'col')), may hold values from 0 to 2
- patterns: int32 [3, 48, 48], replicated, may hold values 0 or 1
Outputs:
- density_next: float32 [6144, 6144], P('row', 'col')
- response_next: float32 [6144, 6144], P('row', 'col')
Inputs may be any that keep to these rules, and one draw needn't show every extreme that they name: `dest_device`: of the 128 strips of one device, at most 2 name the same owner, and some owner is named that often.
All inputs are finite; a program needn't handle non-finite values.
Results may differ from a plain program's by a relative error of at most 0.0036.
Values may be sent and summed in bfloat16 or wider, within the bound.
A program may use at most 128 MiB of HBM per device.

v0:
```python
import math
import jax
import jax.numpy as jnp
from jax import lax
from jax.sharding import PartitionSpec as P

STEPS = 2
CAPACITY = 2


def tile_kept(patterns, which, row_offset, col_offset, block_rows, block_cols, block_width):
    window = lax.dynamic_slice(patterns[which], (row_offset, col_offset), (block_rows, block_cols))
    global_rows = row_offset + lax.iota(jnp.int32, block_rows)
    global_cols = col_offset + lax.iota(jnp.int32, block_cols)
    diagonal = (global_rows[:, None] == global_cols[None, :]).astype(jnp.int32)
    kept = jnp.maximum(window, diagonal).astype(jnp.float32)
    return jnp.repeat(jnp.repeat(kept, block_width, axis=0), block_width, axis=1)


def products(zeroth, linear):
    col_zero, col_first = (
        lax.all_gather(zeroth, "row", axis=0, tiled=True),
        lax.all_gather(linear, "row", axis=0, tiled=True),
    )
    pieces = (
        lax.all_gather(zeroth, "col", axis=1, tiled=True),
        lax.all_gather(linear, "col", axis=1, tiled=True),
    )
    square = jnp.dot(pieces[0], col_zero, preferred_element_type=jnp.float32)
    left_part = jnp.dot(pieces[0], col_first, preferred_element_type=jnp.float32)
    right_part = jnp.dot(pieces[1], col_zero, preferred_element_type=jnp.float32)
    return (square, left_part + right_part)


def on_device(density, strips, dest_device, atom_slot, block_slot, patterns):
    tile_rows, tile_cols = density.shape
    mesh_rows = lax.axis_size("row")
    mesh_cols = lax.axis_size("col")
    devices = mesh_rows * mesh_cols
    matrix_order = tile_rows * mesh_rows
    atom_width = strips.shape[1]
    block_width = strips.shape[2]
    block_rows = tile_rows // block_width
    block_cols = tile_cols // block_width
    row_offset = lax.axis_index("row") * block_rows
    col_offset = lax.axis_index("col") * block_cols
    kept_zero = tile_kept(patterns, 0, row_offset, col_offset, block_rows, block_cols, block_width)
    kept_first = tile_kept(patterns, 1, row_offset, col_offset, block_rows, block_cols, block_width)
    kept_field = tile_kept(patterns, 2, row_offset, col_offset, block_rows, block_cols, block_width)
    capacity = CAPACITY
    targets = dest_device[:, 0]
    order = lax.iota(jnp.int32, targets.shape[0])
    earlier = (targets[:, None] == targets[None, :]) & (order[None, :] < order[:, None])
    ranking = jnp.sum(earlier.astype(jnp.int32), axis=1)
    position = targets * capacity + ranking
    sent_strips = (
        jnp.zeros((devices * capacity, atom_width, block_width), strips.dtype)
        .at[position]
        .set(strips)
    )
    sent_atoms = jnp.full((devices * capacity,), -1, jnp.int32).at[position].set(atom_slot)
    sent_blocks = jnp.zeros((devices * capacity,), jnp.int32).at[position].set(block_slot)
    arrived = (
        lax.all_to_all(
            sent_strips.reshape(devices, capacity, atom_width, block_width),
            ("row", "col"),
            split_axis=0,
            concat_axis=0,
            tiled=True,
        ),
        lax.all_to_all(
            sent_atoms.reshape(devices, capacity),
            ("row", "col"),
            split_axis=0,
            concat_axis=0,
            tiled=True,
        ),
        lax.all_to_all(
            sent_blocks.reshape(devices, capacity),
            ("row", "col"),
            split_axis=0,
            concat_axis=0,
            tiled=True,
        ),
    )
    recv_strips = arrived[0].reshape(-1, atom_width * block_width)
    recv_atoms = arrived[1].reshape(-1)
    recv_blocks = arrived[2].reshape(-1)
    atoms_here = tile_rows // atom_width
    atom_match = recv_atoms[:, None] == lax.iota(jnp.int32, atoms_here)[None, :]
    block_match = recv_blocks[:, None] == lax.iota(jnp.int32, block_cols)[None, :]
    placing = (
        (atom_match[:, :, None] & block_match[:, None, :])
        .astype(jnp.bfloat16)
        .reshape(-1, atoms_here * block_cols)
    )
    summed = lax.dot_general(
        placing, recv_strips, (((0,), (0,)), ((), ())), preferred_element_type=jnp.float32
    )
    h_field = (
        summed.reshape(atoms_here, block_cols, atom_width, block_width)
        .transpose(0, 2, 1, 3)
        .reshape(tile_rows, tile_cols)
    )
    linear = (-(kept_field * h_field)).astype(jnp.bfloat16)
    zeroth = density
    inv_root = 1.0 / math.sqrt(matrix_order)
    new_zeroth = None
    new_linear = None
    for iteration in range(STEPS):
        square, crossed = products(zeroth, linear)
        if iteration % 2 == 0:
            new_zeroth = kept_zero * (square * inv_root)
            new_linear = kept_first * (crossed * inv_root)
        else:
            new_zeroth = kept_zero * (2.0 * zeroth.astype(jnp.float32) - square * inv_root)
            new_linear = kept_first * (2.0 * linear.astype(jnp.float32) - crossed * inv_root)
        zeroth = new_zeroth.astype(jnp.bfloat16)
        linear = new_linear.astype(jnp.bfloat16)
    return (new_zeroth, new_linear)


def solution(mesh):
    return jax.shard_map(
        on_device,
        mesh=mesh,
        in_specs=(
            P("row", "col"),
            P(("row", "col"), None, None),
            P(("row", "col"), None),
            P(("row", "col")),
            P(("row", "col")),
            P(),
        ),
        out_specs=(P("row", "col"), P("row", "col")),
        check_vma=False,
    )
```

profile of v0, /device:TPU:0, one launch (start us, length us, event | category | flops | bytes accessed | tf_op | source)
XLA Modules:
  0.0 540.9 jit_solution(16579620292933018582)
XLA Ops:
  7.2 0.7 all-gather.11.cloned.1.call-update
  7.9 0.9 convert_reduce_fusion
  8.8 0.7 fusion.18
  9.5 1.1 scatter_custom_fusion.1
  10.6 0.8 all_to_all.17
  11.4 11.1 %all-to-all-start.1 = ((s32[128,1,2]{2,1,0:T(1,128)}), s32[128,1,2]{2,1,0:T(1,128)S(1)}, u32[]{:S(2)}, u32[]{:S(2)}) async-start(s32[128,1,2]{2,1,0:T(1,128)} %bitcast.10), calls=%async_computation.1 | async-start | bytes 131072 | tf_op jit(solution)/shard_map/all_to_all | solution.py:78
  22.5 0.8 fusion.23
  23.4 0.1 constant_dynamic-slice_fusion
  23.4 0.1 copy.44
  23.5 0.1 copy.45
  23.6 0.1 constant_dynamic-slice_fusion.2
  23.7 0.1 copy.41
  23.8 0.1 fusion.17
  23.9 1.1 scatter_custom_fusion
  25.0 0.8 all_to_all.15
  25.8 6.5 %all-to-all-done.1 = s32[128,1,2]{2,1,0:T(1,128)S(1)} async-done(((s32[128,1,2]{2,1,0:T(1,128)}), s32[128,1,2]{2,1,0:T(1,128)S(1)}, u32[]{:S(2)}, u32[]{:S(2)}) %all-to-all-start.1) | async-done | bytes 1056 | tf_op jit(solution)/shard_map/all_to_all | solution.py:78
  32.2 4.6 all-to-all-start
  36.8 0.1 broadcast_bitcast_fusion
  36.9 0.9 broadcast_in_dim.50
  37.8 13.4 %scatter_fusion = bf16[256,8,128]{2,1,0:T(8,128)(2,1)} fusion(bf16[256,8,128]{2,1,0:T(8,128)(2,1)} %broadcast_in_dim.50, s32[128]{0:T(128)S(1)} %fusion.18, bf16[128,8,128]{2,1,0:T(8,128)(2,1)S(1)} %copy-done.2), kind=kCustom, calls=%fused_computation.2 | custom fusion | bytes 786944 | tf_op jit(solution)/shard_map/scatter | solution.py:59
  51.1 0.5 broadcast.64
  51.7 0.8 reduce.6
  52.5 0.1 eq.91
  52.6 9.7 %all-to-all-start.2 = ((bf16[128,2,8,128]{3,2,1,0:T(8,128)(2,1)}), bf16[128,2,8,128]{3,2,1,0:T(8,128)(2,1)S(1)}, u32[]{:S(2)}, u32[]{:S(2)}) async-start(bf16[128,2,8,128]{3,2,1,0:T(8,128)(2,1)} %bitcast.13), calls=%async_computation.2 | async-start | bytes 1048576 | tf_op jit(solution)/shard_map/all_to_all | solution.py:64
  62.3 0.0 all-gather.19.cloned.1.call-start
  62.4 0.8 reduce.7
  63.2 0.1 eq.87
  63.3 0.1 broadcast_and_fusion
  63.5 0.1 and.26
  63.6 0.1 dot_general.34
  63.7 12.2 %all-to-all-done.2 = bf16[128,2,8,128]{3,2,1,0:T(8,128)(2,1)S(1)} async-done(((bf16[128,2,8,128]{3,2,1,0:T(8,128)(2,1)}), bf16[128,2,8,128]{3,2,1,0:T(8,128)(2,1)S(1)}, u32[]{:S(2)}, u32[]{:S(2)}) %all-to-all-start.2) | async-done | bytes 524320 | tf_op jit(solution)/shard_map/all_to_all | solution.py:64
  75.9 0.1 copy.71
  76.0 0.2 copy.48
  76.2 0.4 convolution_bitcast_fusion.1
  76.6 0.7 copy.70
  77.3 0.4 copy.51
  77.7 0.9 fusion.12
  78.6 0.0 all-gather.17.cloned.1.call-start
  78.7 0.7 all-gather.17.cloned.1.call-update
  79.4 0.5 all-gather.9.cloned.1.call-update
  79.9 0.0 all-gather.21.cloned.1.call-start
  80.0 0.1 broadcast_bitcast_fusion.1
  80.0 0.1 broadcast_in_dim.21
  80.1 0.4 copy.54
  80.5 69.7 %all-gather.19.cloned.1.call-done = bf16[768,6144]{0,1:T(8,128)(2,1)} async-done(((bf16[768,384]{0,1:T(8,128)(2,1)}), bf16[768,6144]{0,1:T(8,128)(2,1)}) %all-gather.19.cloned.1.call-update) | async-done | bytes 9437200 | tf_op jit(solution)/shard_map/all_gather | solution.py:27
  150.2 9.0 %fusion.24 = f32[768,384]{1,0:T(8,128)S(1)} fusion(bf16[768,6144]{0,1:T(8,128)(2,1)} %all-gather.19.cloned.1.call-done, bf16[6144,384]{1,0:T(8,128)(2,1)} %all-gather.11.cloned.1.call-done), kind=kOutput, calls=%fused_computation.56 | convolution fusion | flops 3623878656 | bytes 15335424 | tf_op jit(solution)/shard_map/dot_general | solution.py:31
  159.3 27.1 %all-gather.17.cloned.1.call-done = bf16[6144,384]{0,1:T(8,128)(2,1)} async-done(((bf16[768,384]{0,1:T(8,128)(2,1)}), bf16[6144,384]{0,1:T(8,128)(2,1)}) %all-gather.17.cloned.1.call-update) | async-done | bytes 4718608 | tf_op jit(solution)/shard_map/all_gather | solution.py:23
  186.4 85.9 %all-gather.9.cloned.1.call-done = bf16[768,6144]{1,0:T(8,128)(2,1)} async-done(((bf16[768,384]{1,0:T(8,128)(2,1)}), bf16[768,6144]{1,0:T(8,128)(2,1)}) %all-gather.9.cloned.1.call-update) | async-done | bytes 9437200 | tf_op jit(solution)/shard_map/all_gather | solution.py:26
  272.2 9.8 %fusion.9 = bf16[768,384]{1,0:T(8,128)(2,1)} fusion(f32[768,384]{1,0:T(8,128)S(1)} %copy.54, f32[768,384]{1,0:T(8,128)S(1)} %fusion.24, bf16[6144,384]{0,1:T(8,128)(2,1)} %all-gather.17.cloned.1.call-done, bf16[768,6144]{1,0:T(8,128)(2,1)} %all-gather.9.cloned.1.call-done), kind=kOutput, calls=%fused_computation.17 | convolution fusion | flops 3625058304 | bytes 17104896 | tf_op jit(solution)/shard_map/dot_general | solution.py:30
  282.1 0.2 all-gather.13.cloned.1.call-start
  282.3 0.1 broadcast_bitcast_fusion.2
  282.4 0.1 broadcast_in_dim.19
  282.5 0.4 copy.43
  282.8 9.7 %fusion.10 = bf16[768,384]{1,0:T(8,128)(2,1)} fusion(f32[768,384]{1,0:T(8,128)S(1)} %copy.43, bf16[768,6144]{1,0:T(8,128)(2,1)} %all-gather.9.cloned.1.call-done, bf16[6144,384]{1,0:T(8,128)(2,1)} %all-gather.11.cloned.1.call-done), kind=kOutput, calls=%fused_computation.18 | convolution fusion | flops 3624763392 | bytes 15925248 | tf_op jit(solution)/shard_map/dot_general | solution.py:29
  292.6 0.0 all-gather.15.cloned.1.call-start
  292.6 0.7 all-gather.15.cloned.1.call-update
  293.4 0.7 all-gather.23.cloned.1.call-update
  294.1 21.6 %all-gather.21.cloned.1.call-done = bf16[6144,384]{1,0:T(8,128)(2,1)} async-done(((bf16[768,384]{1,0:T(8,128)(2,1)}), bf16[6144,384]{1,0:T(8,128)(2,1)}) %all-gather.21.cloned.1.call-update) | async-done | bytes 4718608 | tf_op jit(solution)/shard_map/all_gather | solution.py:23
  315.7 86.4 %all-gather.13.cloned.1.call-done = bf16[768,6144]{1,0:T(8,128)(2,1)} async-done(((bf16[768,384]{1,0:T(8,128)(2,1)}), bf16[768,6144]{1,0:T(8,128)(2,1)}) %all-gather.13.cloned.1.call-update) | async-done | bytes 9437200 | tf_op jit(solution)/shard_map/all_gather | solution.py:26
  402.2 9.8 %fusion.25 = f32[768,384]{1,0:T(8,128)} fusion(bf16[768,6144]{1,0:T(8,128)(2,1)} %all-gather.13.cloned.1.call-done, bf16[6144,384]{1,0:T(8,128)(2,1)} %all-gather.21.cloned.1.call-done), kind=kOutput, calls=%fused_computation.57 | convolution fusion | flops 3623878656 | bytes 15335424 | tf_op jit(solution)/shard_map/dot_general | solution.py:30
  411.9 26.0 %all-gather.15.cloned.1.call-done = bf16[6144,384]{1,0:T(8,128)(2,1)} async-done(((bf16[768,384]{1,0:T(8,128)(2,1)}), bf16[6144,384]{1,0:T(8,128)(2,1)}) %all-gather.15.cloned.1.call-update) | async-done | bytes 4718608 | tf_op jit(solution)/shard_map/all_gather | solution.py:22
  438.0 9.8 %fusion.2 = f32[768,384]{1,0:T(8,128)} fusion(f32[768,384]{1,0:T(8,128)S(1)} %copy.43, bf16[768,6144]{1,0:T(8,128)(2,1)} %all-gather.13.cloned.1.call-done, bf16[6144,384]{1,0:T(8,128)(2,1)} %all-gather.15.cloned.1.call-done, bf16[768,384]{1,0:T(8,128)(2,1)S(1)} %copy-done.1), kind=kOutput, calls=%fused_computation.9 | convolution fusion | flops 3625353216 | bytes 17104896 | tf_op jit(solution)/shard_map/dot_general | solution.py:29
  447.8 76.2 %all-gather.23.cloned.1.call-done = bf16[768,6144]{1,0:T(8,128)(2,1)} async-done(((bf16[768,384]{1,0:T(8,128)(2,1)}), bf16[768,6144]{1,0:T(8,128)(2,1)}) %all-gather.23.cloned.1.call-update) | async-done | bytes 9437200 | tf_op jit(solution)/shard_map/all_gather | solution.py:27
  524.0 10.1 %fusion.8 = f32[768,384]{1,0:T(8,128)} fusion(f32[768,384]{1,0:T(8,128)S(1)} %copy.54, f32[768,384]{1,0:T(8,128)} %fusion.25, bf16[768,6144]{1,0:T(8,128)(2,1)} %all-gather.23.cloned.1.call-done, bf16[6144,384]{1,0:T(8,128)(2,1)} %all-gather.15.cloned.1.call-done, bf16[768,384]{1,0:T(8,128)(2,1)S(1)} %copy-done), kind=kOutput, calls=%fused_computation.16 | convolution fusion | flops 3625648128 | bytes 18284544 | tf_op jit(solution)/shard_map/dot_general | solution.py:31
  (21 shorter events, 0.3 us)
Async XLA Ops:
  7.2 30.6 %copy-start.2 = (bf16[128,8,128]{2,1,0:T(8,128)(2,1)S(1)}, bf16[128,8,128]{2,1,0:T(8,128)(2,1)}, u32[]{:S(2)}) copy-start(bf16[128,8,128]{2,1,0:T(8,128)(2,1)} %param.7) | copy-start | bytes 786436
  7.2 73.4 %all-gather.11.cloned.1.call-start = ((), (), s32[]{:S(2)}) async-start(), calls=%async_computation.4 | async-start | bytes 5308416 | tf_op jit(solution)/shard_map/all_gather | solution.py:22
  11.4 20.8 %all-to-all-start.1 = ((s32[128,1,2]{2,1,0:T(1,128)}), s32[128,1,2]{2,1,0:T(1,128)S(1)}, u32[]{:S(2)}, u32[]{:S(2)}) async-start(s32[128,1,2]{2,1,0:T(1,128)} %bitcast.10), calls=%async_computation.1 | async-start | bytes 131072 | tf_op jit(solution)/shard_map/all_to_all | solution.py:78
  32.2 20.4 %all-to-all-start = ((s32[128,1,2]{2,1,0:T(1,128)}), s32[128,1,2]{2,1,0:T(1,128)S(1)}, u32[]{:S(2)}, u32[]{:S(2)}) async-start(s32[128,1,2]{2,1,0:T(1,128)} %bitcast.9), calls=%async_computation | async-start | bytes 131072 | tf_op jit(solution)/shard_map/all_to_all | solution.py:71
  52.6 23.3 %all-to-all-start.2 = ((bf16[128,2,8,128]{3,2,1,0:T(8,128)(2,1)}), bf16[128,2,8,128]{3,2,1,0:T(8,128)(2,1)S(1)}, u32[]{:S(2)}, u32[]{:S(2)}) async-start(bf16[128,2,8,128]{3,2,1,0:T(8,128)(2,1)} %bitcast.13), calls=%async_computation.2 | async-start | bytes 1048576 | tf_op jit(solution)/shard_map/all_to_all | solution.py:64
  62.3 87.9 %all-gather.19.cloned.1.call-start = ((), (), s32[]{:S(2)}) async-start(), calls=%async_computation.8 | async-start | bytes 10027008 | tf_op jit(solution)/shard_map/all_gather | solution.py:27
  78.6 107.8 %all-gather.17.cloned.1.call-start = ((), (), s32[]{:S(2)}) async-start(), calls=%async_computation.7 | async-start | bytes 5308416 | tf_op jit(solution)/shard_map/all_gather | solution.py:23
  79.3 192.9 %all-gather.9.cloned.1.call-start = ((), (), s32[]{:S(2)}) async-start(), calls=%async_computation.3 | async-start | bytes 10027008 | tf_op jit(solution)/shard_map/all_gather | solution.py:26
  79.9 235.8 %all-gather.21.cloned.1.call-start = ((), (), s32[]{:S(2)}) async-start(), calls=%async_computation.9 | async-start | bytes 5308416 | tf_op jit(solution)/shard_map/all_gather | solution.py:23
  282.1 120.1 %all-gather.13.cloned.1.call-start = ((), (), s32[]{:S(2)}) async-start(), calls=%async_computation.5 | async-start | bytes 10027008 | tf_op jit(solution)/shard_map/all_gather | solution.py:26
  292.6 145.4 %all-gather.15.cloned.1.call-start = ((), (), s32[]{:S(2)}) async-start(), calls=%async_computation.6 | async-start | bytes 5308416 | tf_op jit(solution)/shard_map/all_gather | solution.py:22
  293.3 230.6 %all-gather.23.cloned.1.call-start = ((), (), s32[]{:S(2)}) async-start(), calls=%async_computation.10 | async-start | bytes 10027008 | tf_op jit(solution)/shard_map/all_gather | solution.py:27
  294.1 143.9 %copy-start.1 = (bf16[768,384]{1,0:T(8,128)(2,1)S(1)}, bf16[768,384]{1,0:T(8,128)(2,1)}, u32[]{:S(2)}) copy-start(bf16[768,384]{1,0:T(8,128)(2,1)} %fusion.10) | copy-start | bytes 1769476
  411.9 112.0 %copy-start = (bf16[768,384]{1,0:T(8,128)(2,1)S(1)}, bf16[768,384]{1,0:T(8,128)(2,1)}, u32[]{:S(2)}) copy-start(bf16[768,384]{1,0:T(8,128)(2,1)} %fusion.9) | copy-start | bytes 1769476
Sparse Core Ops, SparseCore 0:
  9.7 37.7 all-gather.10
  78.7 71.4 all-gather.18
  152.5 33.8 all-gather.16
  188.4 83.8 all-gather.8
  282.2 33.4 all-gather.20
  318.3 83.8 all-gather.12
  404.4 33.4 all-gather.14
  440.1 83.8 all-gather.22
where the time goes:
time: 541 us
  waiting for transfers between devices  415 us (77%)
  matrix products  58.5 us (11%)
  starting transfers between devices  25.9 us (5%)
  local copies, waits for them, and re-layouts  22.8 us (4%)
  between operations  14.4 us (3%)
    all_gather x2, waiting for transfers between devices, products(): lax.all_gather(zeroth, 'col', axis=1, tiled=True)  172 us
    all_gather x2, waiting for transfers between devices, products(): lax.all_gather(linear, 'col', axis=1, tiled=True)  146 us
    all_gather x2, waiting for transfers between devices, products(): lax.all_gather(linear, 'row', axis=0, tiled=True)  48.8 us
    all_gather x2, waiting for transfers between devices, products(): lax.all_gather(zeroth, 'row', axis=0, tiled=True)  26 us
    dot_general x2, matrix products, products(): jnp.dot(pieces[0], col_first, preferred_element_type=jnp.float32)  19.6 us
    dot_general x2, matrix products, products(): square = jnp.dot(pieces[0], col_zero, preferred_element_type=jnp.float32)  19.5 us
    dot_general x2, matrix products, products(): jnp.dot(pieces[1], col_zero, preferred_element_type=jnp.float32)  19.1 us
    scatter x1, local copies, waits for them, and re-layouts, on_device(): sent_strips = jnp.zeros((devices * capacity, atom_width, block_width), st...  13.4 us
  transfers between devices with their start and end apart: 11, of which 9 were waited for; matrix products, arithmetic and copies ran while one was open for 12% of the time, Pallas kernels for 0%

commit v1 on v0

--- a/solution.py
+++ b/solution.py
@@ -18,9 +18,37 @@
 
 
 def products(zeroth, linear):
+
+    def show_the_slabs(my_data, shard_axis, which_dim):
+        met_up = lax.psum(1, shard_axis)
+        clean = lax.axis_index(shard_axis)
+        raw_out, all_values, frame_out = (met_up, clean, my_data.shape[which_dim])
+        arrivals = [(w, (w + 1) % raw_out) for w in range(raw_out)]
+        panels = [(w, (w - 1) % raw_out) for w in range(raw_out)]
+        block_next = jnp.zeros(
+            (*my_data.shape[:which_dim], raw_out * frame_out, *my_data.shape[which_dim + 1 :]),
+            my_data.dtype,
+        )
+        block_next = lax.dynamic_update_slice_in_dim(
+            block_next, my_data, all_values * frame_out, axis=which_dim
+        )
+        carry_out = part_next = my_data
+        vec_out = raw_out // 2
+        for kk in range(1, vec_out + 1):
+            carry_out = lax.ppermute(carry_out, shard_axis, arrivals)
+            block_next = lax.dynamic_update_slice_in_dim(
+                block_next, carry_out, (all_values - kk) % raw_out * frame_out, axis=which_dim
+            )
+            if kk < raw_out - vec_out:
+                part_next = lax.ppermute(part_next, shard_axis, panels)
+                block_next = lax.dynamic_update_slice_in_dim(
+                    block_next, part_next, (all_values + kk) % raw_out * frame_out, axis=which_dim
+                )
+        return block_next
+
     col_zero, col_first = (
         lax.all_gather(zeroth, "row", axis=0, tiled=True),
-        lax.all_gather(linear, "row", axis=0, tiled=True),
+        show_the_slabs(linear, "row", 0),
     )
     pieces = (
         lax.all_gather(zeroth, "col", axis=1, tiled=True),

time: 541 us -> 454 us (0.84)
  waiting for transfers between devices: 415 us -> 283 us
  local copies, waits for them, and re-layouts: 22.8 us -> 49.6 us
  starting transfers between devices: 25.9 us -> 44.1 us
    all_gather x2, waiting for transfers between devices: 172 us -> 112 us  [products(): lax.all_gather(zeroth, 'col', axis=1, tiled=True)]
    ppermute x0 -> x14, waiting for transfers between devices: none -> 52.4 us  [the longest x8 52.4 us: show_the_slabs(): carry_out = lax.ppermute(carry_out, shard_axis, arrivals)]
    all_gather x2 -> x0, waiting for transfers between devices: 48.8 us -> none  [products(): lax.all_gather(linear, 'row', axis=0, tiled=True)]
    all_gather x2, waiting for transfers between devices: 146 us -> 98.6 us  [products(): lax.all_gather(linear, 'col', axis=1, tiled=True)]
    all_gather x2, waiting for transfers between devices: 26 us -> 0.02 us  [products(): lax.all_gather(zeroth, 'row', axis=0, tiled=True)]
    ppermute x0 -> x14, starting transfers between devices: none -> 18.2 us  [the longest x6 18.1 us: show_the_slabs(): part_next = lax.ppermute(part_next, shard_axis, panels)]
    dynamic_update_slice x0 -> x15, local copies, waits for them, and re-layouts: none -> 13.4 us  [the longest x8 7.13 us: show_the_slabs(): lax.dynamic_update_slice_in_dim(block_next, carry_out, (all_values - kk)...]
    ppermute x0 -> x7, local copies, waits for them, and re-layouts: none -> 6.41 us  [the longest x3 4.11 us: show_the_slabs(): part_next = lax.ppermute(part_next, shard_axis, panels)]
  transfers between devices with their start and end apart: 11 -> 23, of which waited for: 9 -> 13; matrix products, arithmetic and copies ran while one was open for 12% -> 20% of each run, Pallas kernels for 0% -> 0%
where the time goes in v1:
time: 454 us; the launch traced here: 453 us
  waiting for transfers between devices  283 us (62%)
  matrix products  57 us (13%)
  local copies, waits for them, and re-layouts  49.6 us (11%)
  starting transfers between devices  44.1 us (10%)
  between operations  14.4 us (3%)
    all_gather x2, waiting for transfers between devices, products(): lax.all_gather(zeroth, 'col', axis=1, tiled=True)  112 us
    all_gather x2, waiting for transfers between devices, products(): lax.all_gather(linear, 'col', axis=1, tiled=True)  98.6 us
    ppermute x8, waiting for transfers between devices, show_the_slabs(): carry_out = lax.ppermute(carry_out, shard_axis, arrivals)  52.4 us
    dot_general x2, matrix products, products(): square = jnp.dot(pieces[0], col_zero, preferred_element_type=jnp.float32)  19.5 us
    dot_general x2, matrix products, products(): jnp.dot(pieces[0], col_first, preferred_element_type=jnp.float32)  18.8 us
    dot_general x2, matrix products, products(): jnp.dot(pieces[1], col_zero, preferred_element_type=jnp.float32)  18.4 us
    ppermute x6, starting transfers between devices, show_the_slabs(): part_next = lax.ppermute(part_next, shard_axis, panels)  18.1 us
    scatter x1, local copies, waits for them, and re-layouts, on_device(): sent_strips = jnp.zeros((devices * capacity, atom_width, block_width), st...  14 us
  transfers between devices with their start and end apart: 23, of which 13 were waited for; matrix products, arithmetic and copies ran while one was open for 20% of the time, Pallas kernels for 0%

profile of v1, /device:TPU:0, one launch (start us, length us, event | category | flops | bytes accessed | tf_op | source)
XLA Modules:
  0.0 452.6 jit_solution(7118370819507254357)
XLA Ops:
  7.2 0.7 all-gather.9.cloned.1.call-update
  7.9 0.7 all-gather.7.cloned.1.call-update
  8.6 0.9 convert_reduce_fusion
  10.2 1.1 scatter_custom_fusion.1
  11.3 0.8 all_to_all.17
  12.1 11.1 %all-to-all-start.1 = ((s32[128,1,2]{2,1,0:T(1,128)}), s32[128,1,2]{2,1,0:T(1,128)S(1)}, u32[]{:S(2)}, u32[]{:S(2)}) async-start(s32[128,1,2]{2,1,0:T(1,128)} %bitcast.10), calls=%async_computation.1 | async-start | bytes 131072 | tf_op jit(solution)/shard_map/all_to_all | solution.py:106
  23.3 0.8 fusion.23
  24.6 1.1 scatter_custom_fusion
  25.7 0.8 all_to_all.15
  26.5 6.2 %all-to-all-done.1 = s32[128,1,2]{2,1,0:T(1,128)S(1)} async-done(((s32[128,1,2]{2,1,0:T(1,128)}), s32[128,1,2]{2,1,0:T(1,128)S(1)}, u32[]{:S(2)}, u32[]{:S(2)}) %all-to-all-start.1) | async-done | bytes 1056 | tf_op jit(solution)/shard_map/all_to_all | solution.py:106
  32.7 4.6 %all-to-all-start = ((s32[128,1,2]{2,1,0:T(1,128)}), s32[128,1,2]{2,1,0:T(1,128)S(1)}, u32[]{:S(2)}, u32[]{:S(2)}) async-start(s32[128,1,2]{2,1,0:T(1,128)} %bitcast.9), calls=%async_computation | async-start | bytes 131072 | tf_op jit(solution)/shard_map/all_to_all | solution.py:99
  37.3 0.9 broadcast_in_dim.50
  38.2 14.0 %scatter_fusion = bf16[256,8,128]{2,1,0:T(8,128)(2,1)} fusion(bf16[256,8,128]{2,1,0:T(8,128)(2,1)} %broadcast_in_dim.50, s32[128]{0:T(128)S(1)} %fusion.18, bf16[128,8,128]{2,1,0:T(8,128)(2,1)} %param.7), kind=kCustom, calls=%fused_computation.2 | custom fusion | bytes 786944 | tf_op jit(solution)/shard_map/scatter | solution.py:87
  52.7 0.8 reduce.6
  53.6 9.8 %all-to-all-start.2 = ((bf16[128,2,8,128]{3,2,1,0:T(8,128)(2,1)}), bf16[128,2,8,128]{3,2,1,0:T(8,128)(2,1)S(1)}, u32[]{:S(2)}, u32[]{:S(2)}) async-start(bf16[128,2,8,128]{3,2,1,0:T(8,128)(2,1)} %bitcast.13), calls=%async_computation.2 | async-start | bytes 1048576 | tf_op jit(solution)/shard_map/all_to_all | solution.py:92
  63.5 0.8 reduce.7
  64.8 12.2 %all-to-all-done.2 = bf16[128,2,8,128]{3,2,1,0:T(8,128)(2,1)S(1)} async-done(((bf16[128,2,8,128]{3,2,1,0:T(8,128)(2,1)}), bf16[128,2,8,128]{3,2,1,0:T(8,128)(2,1)S(1)}, u32[]{:S(2)}, u32[]{:S(2)}) %all-to-all-start.2) | async-done | bytes 524320 | tf_op jit(solution)/shard_map/all_to_all | solution.py:92
  77.7 0.7 copy.94
  78.8 0.9 fusion.12
  80.4 58.2 %all-gather.7.cloned.1.call-done = bf16[768,6144]{1,0:T(8,128)(2,1)} async-done(((bf16[768,384]{1,0:T(8,128)(2,1)}), bf16[768,6144]{1,0:T(8,128)(2,1)}) %all-gather.7.cloned.1.call-update) | async-done | bytes 9437200 | tf_op jit(solution)/shard_map/all_gather | solution.py:54
  138.6 9.7 %fusion.10 = bf16[768,384]{1,0:T(8,128)(2,1)} fusion(f32[768,384]{1,0:T(8,128)S(1)} %copy.59, bf16[768,6144]{1,0:T(8,128)(2,1)} %all-gather.7.cloned.1.call-done, bf16[6144,384]{1,0:T(8,128)(2,1)} %all-gather.9.cloned.1.call-done), kind=kOutput, calls=%fused_computation.18 | convolution fusion | flops 3624763392 | bytes 15925248 | tf_op jit(solution)/shard_map/dot_general | solution.py:57
  149.2 2.9 collective-permute-start.1
  152.1 7.6 %collective-permute-done = bf16[768,384]{0,1:T(8,128)(2,1)S(1)} collective-permute-done((bf16[768,384]{0,1:T(8,128)(2,1)S(1)}, bf16[768,384]{0,1:T(8,128)(2,1)S(1)}, u32[]{:S(2)}, u32[]{:S(2)}) %collective-permute-start) | collective-permute-done | bytes 589856 | tf_op jit(solution)/shard_map/ppermute | solution.py:38
  159.7 3.3 collective-permute-start.3
  163.0 7.3 %collective-permute-done.2 = bf16[768,384]{0,1:T(8,128)(2,1)} collective-permute-done((bf16[768,384]{0,1:T(8,128)(2,1)S(1)}, bf16[768,384]{0,1:T(8,128)(2,1)}, u32[]{:S(2)}, u32[]{:S(2)}) %collective-permute-start.2) | collective-permute-done | bytes 589856 | tf_op jit(solution)/shard_map/ppermute | solution.py:38
  170.5 1.4 copy.78
  172.2 3.0 collective-permute-start.5
  175.2 2.5 broadcast.58.clone
  177.7 0.9 constant_dynamic-update-slice_fusion.15
  178.9 1.4 copy.70
  180.3 0.9 constant_dynamic-update-slice_fusion.14
  181.2 0.9 constant_dynamic-update-slice_fusion.13
  182.1 1.4 copy.71
  183.5 1.4 copy.72
  184.9 0.9 constant_dynamic-update-slice_fusion.12
  185.8 0.9 constant_dynamic-update-slice_fusion.11
  187.0 1.4 copy.74
  188.3 0.9 constant_dynamic-update-slice_fusion.10
  189.2 0.9 constant_dynamic-update-slice_fusion.9
  190.2 1.5 collective-permute-done.6
  192.0 0.9 constant_dynamic-update-slice_fusion.8
  192.9 22.8 %all-gather.15.cloned.1.call-done = bf16[768,6144]{0,1:T(8,128)(2,1)} async-done(((bf16[768,384]{0,1:T(8,128)(2,1)}), bf16[768,6144]{0,1:T(8,128)(2,1)}) %all-gather.15.cloned.1.call-update) | async-done | bytes 9437200 | tf_op jit(solution)/shard_map/all_gather | solution.py:55
  215.7 9.0 %fusion.24 = f32[768,384]{1,0:T(8,128)S(1)} fusion(bf16[768,6144]{0,1:T(8,128)(2,1)} %all-gather.15.cloned.1.call-done, bf16[6144,384]{1,0:T(8,128)(2,1)} %all-gather.9.cloned.1.call-done), kind=kOutput, calls=%fused_computation.72 | convolution fusion | flops 3623878656 | bytes 15335424 | tf_op jit(solution)/shard_map/dot_general | solution.py:59
  224.8 2.6 broadcast.58
  227.3 10.3 %constant_dynamic-update-slice_fusion.7 = (bf16[6144,384]{1,0:T(8,128)(2,1)}, bf16[768,384]{1,0:T(8,128)(2,1)}) fusion(bf16[6144,384]{1,0:T(8,128)(2,1)} %broadcast.58, s32[]{:T(128)S(6)} %select_n.96, f32[768,384]{1,0:T(8,128)S(1)} %copy-done.2, f32[768,384]{1,0:T(8,128)S(1)} %fusion.24, bf16[768,6144]{1,0:T(8,128)(2,1)} %all-gather.7.cloned.1.call-done, ...), kind=kOutput, calls=%fused_computation.43 | convolution fusion | flops 3625058304 | bytes 17694724 | tf_op jit(solution)/shard_map/dot_general | solution.py:58
  237.7 2.9 collective-permute-start.8
  240.6 15.7 %collective-permute-done.7 = bf16[768,384]{1,0:T(8,128)(2,1)S(1)} collective-permute-done((bf16[768,384]{1,0:T(8,128)(2,1)}, bf16[768,384]{1,0:T(8,128)(2,1)S(1)}, u32[]{:S(2)}, u32[]{:S(2)}) %collective-permute-start.7) | collective-permute-done | bytes 589856 | tf_op jit(solution)/shard_map/ppermute | solution.py:38
  256.4 3.0 collective-permute-start.10
  259.3 7.6 %collective-permute-done.9 = bf16[768,384]{1,0:T(8,128)(2,1)S(1)} collective-permute-done((bf16[768,384]{1,0:T(8,128)(2,1)S(1)}, bf16[768,384]{1,0:T(8,128)(2,1)S(1)}, u32[]{:S(2)}, u32[]{:S(2)}) %collective-permute-start.9) | collective-permute-done | bytes 589856 | tf_op jit(solution)/shard_map/ppermute | solution.py:38
  266.9 3.0 collective-permute-start.12
  269.8 0.9 constant_dynamic-update-slice_fusion.6
  270.7 6.7 %collective-permute-done.11 = bf16[768,384]{1,0:T(8,128)(2,1)S(1)} collective-permute-done((bf16[768,384]{1,0:T(8,128)(2,1)S(1)}, bf16[768,384]{1,0:T(8,128)(2,1)S(1)}, u32[]{:S(2)}, u32[]{:S(2)}) %collective-permute-start.11) | collective-permute-done | bytes 589856 | tf_op jit(solution)/shard_map/ppermute | solution.py:38
  277.4 0.9 constant_dynamic-update-slice_fusion.5
  278.3 0.9 constant_dynamic-update-slice_fusion.4
  279.2 0.9 constant_dynamic-update-slice_fusion.3
  280.1 0.9 constant_dynamic-update-slice_fusion.2
  280.9 0.9 constant_dynamic-update-slice_fusion.1
  281.8 6.1 %collective-permute-done.13 = bf16[768,384]{1,0:T(8,128)(2,1)S(1)} collective-permute-done((bf16[768,384]{1,0:T(8,128)(2,1)S(1)}, bf16[768,384]{1,0:T(8,128)(2,1)S(1)}, u32[]{:S(2)}, u32[]{:S(2)}) %collective-permute-start.13) | collective-permute-done | bytes 589856 | tf_op jit(solution)/shard_map/ppermute | solution.py:38
  287.9 0.9 constant_dynamic-update-slice_fusion
  288.8 53.4 %all-gather.11.cloned.1.call-done = bf16[768,6144]{1,0:T(8,128)(2,1)} async-done(((bf16[768,384]{1,0:T(8,128)(2,1)}), bf16[768,6144]{1,0:T(8,128)(2,1)}) %all-gather.11.cloned.1.call-update) | async-done | bytes 9437200 | tf_op jit(solution)/shard_map/all_gather | solution.py:54
  342.2 9.8 %fusion.2 = f32[768,384]{1,0:T(8,128)} fusion(f32[768,384]{1,0:T(8,128)S(1)} %copy.59, bf16[768,6144]{1,0:T(8,128)(2,1)} %all-gather.11.cloned.1.call-done, bf16[6144,384]{1,0:T(8,128)(2,1)} %all-gather.13.cloned.1.call-done, bf16[768,384]{1,0:T(8,128)(2,1)S(1)} %copy-done.1), kind=kOutput, calls=%fused_computation.9 | convolution fusion | flops 3625353216 | bytes 17104896 | tf_op jit(solution)/shard_map/dot_general | solution.py:57
  352.1 75.8 %all-gather.17.cloned.1.call-done = bf16[768,6144]{1,0:T(8,128)(2,1)} async-done(((bf16[768,384]{1,0:T(8,128)(2,1)}), bf16[768,6144]{1,0:T(8,128)(2,1)}) %all-gather.17.cloned.1.call-update) | async-done | bytes 9437200 | tf_op jit(solution)/shard_map/all_gather | solution.py:55
  427.9 9.3 %fusion.25 = f32[768,384]{1,0:T(8,128)S(1)} fusion(bf16[768,6144]{1,0:T(8,128)(2,1)} %all-gather.17.cloned.1.call-done, bf16[6144,384]{1,0:T(8,128)(2,1)} %all-gather.13.cloned.1.call-done), kind=kOutput, calls=%fused_computation.73 | convolution fusion | flops 3623878656 | bytes 15335424 | tf_op jit(solution)/shard_map/dot_general | solution.py:59
  437.2 8.5 %fusion.8 = f32[768,384]{1,0:T(8,128)} fusion(f32[768,384]{1,0:T(8,128)S(1)} %copy-done.2, f32[768,384]{1,0:T(8,128)S(1)} %fusion.25, bf16[768,6144]{1,0:T(8,128)(2,1)S(1)} %copy-done.6, bf16[6144,384]{1,0:T(8,128)(2,1)} %constant_dynamic-update-slice_fusion, bf16[768,384]{1,0:T(8,128)(2,1)S(1)} %copy-done.5), kind=kOutput, calls=%fused_computation.16 | convolution fusion | flops 3625648128 | bytes 18284544 | tf_op jit(solution)/shard_map/dot_general | solution.py:58
  (76 shorter events, 6.5 us)
Async XLA Ops:
  7.2 73.2 %all-gather.9.cloned.1.call-start = ((), (), s32[]{:S(2)}) async-start(), calls=%async_computation.4 | async-start | bytes 5308416 | tf_op jit(solution)/shard_map/all_gather | solution.py:50
  7.9 130.7 %all-gather.7.cloned.1.call-start = ((), (), s32[]{:S(2)}) async-start(), calls=%async_computation.3 | async-start | bytes 10027008 | tf_op jit(solution)/shard_map/all_gather | solution.py:54
  12.1 20.6 %all-to-all-start.1 = ((s32[128,1,2]{2,1,0:T(1,128)}), s32[128,1,2]{2,1,0:T(1,128)S(1)}, u32[]{:S(2)}, u32[]{:S(2)}) async-start(s32[128,1,2]{2,1,0:T(1,128)} %bitcast.10), calls=%async_computation.1 | async-start | bytes 131072 | tf_op jit(solution)/shard_map/all_to_all | solution.py:106
  32.7 21.0 %all-to-all-start = ((s32[128,1,2]{2,1,0:T(1,128)}), s32[128,1,2]{2,1,0:T(1,128)S(1)}, u32[]{:S(2)}, u32[]{:S(2)}) async-start(s32[128,1,2]{2,1,0:T(1,128)} %bitcast.9), calls=%async_computation | async-start | bytes 131072 | tf_op jit(solution)/shard_map/all_to_all | solution.py:99
  53.6 23.4 %all-to-all-start.2 = ((bf16[128,2,8,128]{3,2,1,0:T(8,128)(2,1)}), bf16[128,2,8,128]{3,2,1,0:T(8,128)(2,1)S(1)}, u32[]{:S(2)}, u32[]{:S(2)}) async-start(bf16[128,2,8,128]{3,2,1,0:T(8,128)(2,1)} %bitcast.13), calls=%async_computation.2 | async-start | bytes 1048576 | tf_op jit(solution)/shard_map/all_to_all | solution.py:92
  63.4 152.3 %all-gather.15.cloned.1.call-start = ((), (), s32[]{:S(2)}) async-start(), calls=%async_computation.7 | async-start | bytes 10027008 | tf_op jit(solution)/shard_map/all_gather | solution.py:55
  79.8 209.0 %all-gather.13.cloned.1.call-start = ((), (), s32[]{:S(2)}) async-start(), calls=%async_computation.6 | async-start | bytes 5308416 | tf_op jit(solution)/shard_map/all_gather | solution.py:50
  80.3 68.8 %copy-start = (bf16[768,384]{0,1:T(8,128)(2,1)S(1)}, bf16[768,384]{0,1:T(8,128)(2,1)}, u32[]{:S(2)}) copy-start(bf16[768,384]{0,1:T(8,128)(2,1)} %fusion.12) | copy-start | bytes 1769476
  148.3 193.9 %all-gather.11.cloned.1.call-start = ((), (), s32[]{:S(2)}) async-start(), calls=%async_computation.5 | async-start | bytes 10027008 | tf_op jit(solution)/shard_map/all_gather | solution.py:54
  148.9 279.0 %all-gather.17.cloned.1.call-start = ((), (), s32[]{:S(2)}) async-start(), calls=%async_computation.8 | async-start | bytes 10027008 | tf_op jit(solution)/shard_map/all_gather | solution.py:55
  149.2 10.5 %collective-permute-start = (bf16[768,384]{0,1:T(8,128)(2,1)S(1)}, bf16[768,384]{0,1:T(8,128)(2,1)S(1)}, u32[]{:S(2)}, u32[]{:S(2)}) collective-permute-start(bf16[768,384]{0,1:T(8,128)(2,1)S(1)} %copy-done), channel_id=1, source_target_pairs={{0,16},{16,32},{32,48},{48,64},{64,80},{80,96},{96,112},{112,0},{1... | collective-permute-start | bytes 1769480 | tf_op jit(solution)/shard_map/ppermute | solution.py:38
  149.2 10.5 %collective-permute-start.1 = (bf16[768,384]{0,1:T(8,128)(2,1)S(1)}, bf16[768,384]{0,1:T(8,128)(2,1)}, u32[]{:S(2)}, u32[]{:S(2)}) collective-permute-start(bf16[768,384]{0,1:T(8,128)(2,1)S(1)} %copy-done), channel_id=1, source_target_pairs={{0,112},{16,0},{32,16},{48,32},{64,48},{80,64},{96,80},{112,96},{1... | collective-permute-start | bytes 1769480 | tf_op jit(solution)/shard_map/ppermute | solution.py:43
  159.7 10.7 %copy-start.3 = (bf16[768,384]{0,1:T(8,128)(2,1)}, bf16[768,384]{0,1:T(8,128)(2,1)S(1)}, u32[]{:S(2)}) copy-start(bf16[768,384]{0,1:T(8,128)(2,1)S(1)} %collective-permute-done) | copy-start | bytes 1769476
  159.7 10.6 %collective-permute-start.2 = (bf16[768,384]{0,1:T(8,128)(2,1)S(1)}, bf16[768,384]{0,1:T(8,128)(2,1)}, u32[]{:S(2)}, u32[]{:S(2)}) collective-permute-start(bf16[768,384]{0,1:T(8,128)(2,1)S(1)} %collective-permute-done), channel_id=1, source_target_pairs={{0,16},{16,32},{32,48},{48,64},{64,80},{80,96},{96,112},{112,0},{1... | collective-permute-start | bytes 1769480 | tf_op jit(solution)/shard_map/ppermute | solution.py:38
  159.7 12.5 %collective-permute-start.3 = (bf16[768,384]{0,1:T(8,128)(2,1)}, bf16[768,384]{0,1:T(8,128)(2,1)}, u32[]{:S(2)}, u32[]{:S(2)}) collective-permute-start(bf16[768,384]{0,1:T(8,128)(2,1)} %collective-permute-done.1), channel_id=1, source_target_pairs={{0,112},{16,0},{32,16},{48,32},{64,48},{80,64},{96,80},{112,96},{1... | collective-permute-start | bytes 1769480 | tf_op jit(solution)/shard_map/ppermute | solution.py:43
  170.3 10.9 %collective-permute-start.4 = (bf16[768,384]{0,1:T(8,128)(2,1)}, bf16[768,384]{0,1:T(8,128)(2,1)S(1)}, u32[]{:S(2)}, u32[]{:S(2)}) collective-permute-start(bf16[768,384]{0,1:T(8,128)(2,1)} %collective-permute-done.2), channel_id=1, source_target_pairs={{0,16},{16,32},{32,48},{48,64},{64,80},{80,96},{96,112},{112,0},{1... | collective-permute-start | bytes 1769480 | tf_op jit(solution)/shard_map/ppermute | solution.py:38
  171.9 6.7 %copy-start.4 = (bf16[768,384]{0,1:T(8,128)(2,1)S(1)}, bf16[768,384]{0,1:T(8,128)(2,1)}, u32[]{:S(2)}) copy-start(bf16[768,384]{0,1:T(8,128)(2,1)} %copy-done.3) | copy-start | bytes 1769476
  172.2 14.8 %collective-permute-start.5 = (bf16[768,384]{0,1:T(8,128)(2,1)}, bf16[768,384]{0,1:T(8,128)(2,1)}, u32[]{:S(2)}, u32[]{:S(2)}) collective-permute-start(bf16[768,384]{0,1:T(8,128)(2,1)} %collective-permute-done.3), channel_id=1, source_target_pairs={{0,112},{16,0},{32,16},{48,32},{64,48},{80,64},{96,80},{112,96},{1... | collective-permute-start | bytes 1769480 | tf_op jit(solution)/shard_map/ppermute | solution.py:43
  181.2 10.5 %collective-permute-start.6 = (bf16[768,384]{0,1:T(8,128)(2,1)S(1)}, bf16[768,384]{0,1:T(8,128)(2,1)S(1)}, u32[]{:S(2)}, u32[]{:S(2)}) collective-permute-start(bf16[768,384]{0,1:T(8,128)(2,1)S(1)} %collective-permute-done.4), channel_id=1, source_target_pairs={{0,16},{16,32},{32,48},{48,64},{64,80},{80,96},{96,112},{112,0},{1... | collective-permute-start | bytes 1769480 | tf_op jit(solution)/shard_map/ppermute | solution.py:38
  224.7 2.6 copy-start.2
  237.6 104.6 %copy-start.1 = (bf16[768,384]{1,0:T(8,128)(2,1)S(1)}, bf16[768,384]{1,0:T(8,128)(2,1)}, u32[]{:S(2)}) copy-start(bf16[768,384]{1,0:T(8,128)(2,1)} %fusion.10) | copy-start | bytes 1769476
  237.6 18.7 %collective-permute-start.7 = (bf16[768,384]{1,0:T(8,128)(2,1)}, bf16[768,384]{1,0:T(8,128)(2,1)S(1)}, u32[]{:S(2)}, u32[]{:S(2)}) collective-permute-start(bf16[768,384]{1,0:T(8,128)(2,1)} %get-tuple-element.9), channel_id=1, source_target_pairs={{0,16},{16,32},{32,48},{48,64},{64,80},{80,96},{96,112},{112,0},{1... | collective-permute-start | bytes 1769480 | tf_op jit(solution)/shard_map/ppermute | solution.py:38
  237.7 18.7 %collective-permute-start.8 = (bf16[768,384]{1,0:T(8,128)(2,1)}, bf16[768,384]{1,0:T(8,128)(2,1)S(1)}, u32[]{:S(2)}, u32[]{:S(2)}) collective-permute-start(bf16[768,384]{1,0:T(8,128)(2,1)} %get-tuple-element.9), channel_id=1, source_target_pairs={{0,112},{16,0},{32,16},{48,32},{64,48},{80,64},{96,80},{112,96},{1... | collective-permute-start | bytes 1769480 | tf_op jit(solution)/shard_map/ppermute | solution.py:43
  256.3 10.5 %collective-permute-start.9 = (bf16[768,384]{1,0:T(8,128)(2,1)S(1)}, bf16[768,384]{1,0:T(8,128)(2,1)S(1)}, u32[]{:S(2)}, u32[]{:S(2)}) collective-permute-start(bf16[768,384]{1,0:T(8,128)(2,1)S(1)} %collective-permute-done.7), channel_id=1, source_target_pairs={{0,16},{16,32},{32,48},{48,64},{64,80},{80,96},{96,112},{112,0},{1... | collective-permute-start | bytes 1769480 | tf_op jit(solution)/shard_map/ppermute | solution.py:38
  256.4 10.5 %collective-permute-start.10 = (bf16[768,384]{1,0:T(8,128)(2,1)S(1)}, bf16[768,384]{1,0:T(8,128)(2,1)S(1)}, u32[]{:S(2)}, u32[]{:S(2)}) collective-permute-start(bf16[768,384]{1,0:T(8,128)(2,1)S(1)} %collective-permute-done.8), channel_id=1, source_target_pairs={{0,112},{16,0},{32,16},{48,32},{64,48},{80,64},{96,80},{112,96},{1... | collective-permute-start | bytes 1769480 | tf_op jit(solution)/shard_map/ppermute | solution.py:43
  266.9 10.5 %collective-permute-start.11 = (bf16[768,384]{1,0:T(8,128)(2,1)S(1)}, bf16[768,384]{1,0:T(8,128)(2,1)S(1)}, u32[]{:S(2)}, u32[]{:S(2)}) collective-permute-start(bf16[768,384]{1,0:T(8,128)(2,1)S(1)} %collective-permute-done.9), channel_id=1, source_target_pairs={{0,16},{16,32},{32,48},{48,64},{64,80},{80,96},{96,112},{112,0},{1... | collective-permute-start | bytes 1769480 | tf_op jit(solution)/shard_map/ppermute | solution.py:38
  266.9 14.1 %collective-permute-start.12 = (bf16[768,384]{1,0:T(8,128)(2,1)S(1)}, bf16[768,384]{1,0:T(8,128)(2,1)S(1)}, u32[]{:S(2)}, u32[]{:S(2)}) collective-permute-start(bf16[768,384]{1,0:T(8,128)(2,1)S(1)} %collective-permute-done.10), channel_id=1, source_target_pairs={{0,112},{16,0},{32,16},{48,32},{64,48},{80,64},{96,80},{112,96},{1... | collective-permute-start | bytes 1769480 | tf_op jit(solution)/shard_map/ppermute | solution.py:43
  277.4 10.5 %collective-permute-start.13 = (bf16[768,384]{1,0:T(8,128)(2,1)S(1)}, bf16[768,384]{1,0:T(8,128)(2,1)S(1)}, u32[]{:S(2)}, u32[]{:S(2)}) collective-permute-start(bf16[768,384]{1,0:T(8,128)(2,1)S(1)} %collective-permute-done.11), channel_id=1, source_target_pairs={{0,16},{16,32},{32,48},{48,64},{64,80},{80,96},{96,112},{112,0},{1... | collective-permute-start | bytes 1769480 | tf_op jit(solution)/shard_map/ppermute | solution.py:38
  352.1 85.2 %copy-start.5 = (bf16[768,384]{1,0:T(8,128)(2,1)S(1)}, bf16[768,384]{1,0:T(8,128)(2,1)}, u32[]{:S(2)}) copy-start(bf16[768,384]{1,0:T(8,128)(2,1)} %get-tuple-element.9) | copy-start | bytes 1769476
  427.9 9.4 %copy-start.6 = (bf16[768,6144]{1,0:T(8,128)(2,1)S(1)}, bf16[768,6144]{1,0:T(8,128)(2,1)}, u32[]{:S(2)}) copy-start(bf16[768,6144]{1,0:T(8,128)(2,1)} %all-gather.11.cloned.1.call-done) | copy-start | bytes 28311556
Sparse Core Ops, SparseCore 0:
  9.7 38.0 all-gather.8
  49.9 88.6 all-gather.6
  140.8 74.9 all-gather.14
  217.8 37.9 all-gather.12
  258.3 83.8 all-gather.10
  344.8 83.0 all-gather.16
